TPU v7x, 32 devices: a whole 2x2x4 slice. The times are simulated.
32 devices in a mesh: row: 4 (over y, core), col: 4 (over z), dp: 2 (over x).
Axes of the slice: x: 2, y: 2, z: 4, core: 2. Of those that a mesh axis runs over, the one named last changes fastest.
Arguments:
- pair: bfloat16 [2, 64, 512, 512], P('dp', None, 'row', 'col'), may hold values from -120 to 120
- cotangent: bfloat16 [2, 64, 512, 512], P('dp', None, 'row', 'col'), may hold values from -6 to 6
- chain: int32 [2, 512], P('dp'), may hold values from 0 to 3, never falling along the last dimension, each value on 1 to 256 neighbouring positions
- dilation: int32 [2], replicated, may hold values from 1 to 8, as said below
- w_one: bfloat16 [9, 64, 64], replicated, may hold values from -0.25 to 0.25
- w_two: bfloat16 [9, 64, 64], replicated, may hold values from -0.25 to 0.25
- gain_one: float32 [64], replicated, may hold values from 0.25 to 1.75
- gain_two: float32 [64], replicated, may hold values from 0.25 to 1.75
- inter_bias: float32 [64], replicated, may hold values from -4 to 4
Outputs:
- grad_w_one: float32 [9, 64, 64], replicated
- grad_w_two: float32 [9, 64, 64], replicated
- grad_gain_one: float32 [64], replicated
- grad_gain_two: float32 [64], replicated
- grad_inter: float32 [64], replicated
- loss: float32 [], replicated
Inputs may be any that keep to these rules, and one draw needn't show every extreme that they name: `dilation`: each entry is 1, 2, 4 or 8, and at least one entry is 8. chain numbers never fall along a complex's residues; each of the 4 chains has at most 256 residues.
All inputs are finite; a program needn't handle non-finite values.
Results may differ from a plain program's by a relative error of at most 0.0071.
Values may be sent and summed in bfloat16 or wider, within the bound.
A program may use at most 128 MiB of HBM per device.

v0:
```python
import jax
import jax.numpy as jnp
from jax import lax
from jax.sharding import PartitionSpec as P

kernel_reach = 8
eps = 1e-05


def padded(block, sides, width):
    for axis, dim in sides:
        count = lax.axis_size(axis)
        forward = [(i, i + 1) for i in range(count - 1)]
        backward = [(target, source) for source, target in forward]
        low = lax.ppermute(
            lax.slice_in_dim(block, block.shape[dim] - width, None, axis=dim), axis, forward
        )
        high = lax.ppermute(lax.slice_in_dim(block, 0, width, axis=dim), axis, backward)
        block = jnp.concatenate([low, block, high], axis=dim)
    return block


def elu(z):
    return jnp.where(z > 0, z, jnp.exp(jnp.minimum(z, 0.0)) - 1.0)


def elu_slope(z):
    return jnp.where(z > 0, 1.0, jnp.exp(jnp.minimum(z, 0.0)))


def kernel_tap_window(padded_input, first, second, input_shape):
    zero = jnp.int32(0)
    return lax.dynamic_slice(padded_input, (zero, first, second), input_shape)


def widen(values):
    return padded(values, (("row", 1), ("col", 2)), kernel_reach)


def dilated_convolve(padded_input, input_shape, kernel_weights, dilation_rate):
    chans = input_shape[0]
    total = jnp.zeros((chans, input_shape[1] * input_shape[2]), jnp.float32)
    for step in range(9):
        upper_triangle, left_padding = (step // 3 - 1, step % 3 - 1)
        window_slice = kernel_tap_window(
            padded_input,
            kernel_reach + dilation_rate * upper_triangle,
            kernel_reach + dilation_rate * left_padding,
            input_shape,
        )
        total = total + jnp.dot(
            kernel_weights[step],
            window_slice.reshape(chans, -1),
            preferred_element_type=jnp.float32,
        )
    return total.reshape(input_shape)


def convolve_backward(output_gradient, kernel_weights, dilation_rate):
    chans = output_gradient.shape[0]
    padded_input = widen(output_gradient)
    total = jnp.zeros((chans, output_gradient.shape[1] * output_gradient.shape[2]), jnp.float32)
    for step in range(9):
        upper_triangle, left_padding = (step // 3 - 1, step % 3 - 1)
        window_slice = kernel_tap_window(
            padded_input,
            kernel_reach - dilation_rate * upper_triangle,
            kernel_reach - dilation_rate * left_padding,
            output_gradient.shape,
        )
        total = total + jnp.dot(
            kernel_weights[step].T,
            window_slice.reshape(chans, -1),
            preferred_element_type=jnp.float32,
        )
    return total.reshape(output_gradient.shape)


def kernel_weight_gradient(output_gradient, padded_input, dilation_rate):
    chans = output_gradient.shape[0]
    flat = output_gradient.reshape(chans, -1)
    result = []
    for step in range(9):
        upper_triangle, left_padding = (step // 3 - 1, step % 3 - 1)
        window_slice = kernel_tap_window(
            padded_input,
            kernel_reach + dilation_rate * upper_triangle,
            kernel_reach + dilation_rate * left_padding,
            output_gradient.shape,
        )
        result.append(
            lax.dot_general(
                flat,
                window_slice.reshape(chans, -1),
                (((1,), (1,)), ((), ())),
                preferred_element_type=jnp.float32,
            )
        )
    return jnp.stack(result)


def paired_total(first, second):
    return lax.psum((first, second), ("row", "col"))


def normalize(values, count):
    totals = paired_total(jnp.sum(values, axis=(1, 2)), jnp.sum(values * values, axis=(1, 2)))
    mean = totals[0] / count
    var = totals[1] / count - mean * mean
    centred = values - mean[:, None, None]
    return (centred * lax.rsqrt(var + eps)[:, None, None], var)


def local(pair, cotangent, chain, dilation, w_one, w_two, gain_one, gain_two, inter_bias):
    chans, side = (pair.shape[1], pair.shape[2])
    groups = lax.axis_size("row")
    length = side * groups
    count = float(length * length)
    stacked = pair.reshape(1, 1, chans, side, side)
    sectioned = lax.all_to_all(
        lax.all_to_all(stacked, "row", split_axis=3, concat_axis=0, tiled=True),
        "col",
        split_axis=0,
        concat_axis=1,
        tiled=True,
    )
    landed = lax.all_to_all(sectioned, "row", split_axis=1, concat_axis=0, tiled=True)
    pieces = landed.reshape(groups, chans, side // groups, side)
    mirrored = jnp.swapaxes(jnp.transpose(pieces, (1, 0, 2, 3)).reshape(chans, side, side), 1, 2)
    tile = pair[0]
    sym = ((tile.astype(jnp.float32) + mirrored.astype(jnp.float32)) * 0.5).astype(jnp.bfloat16)
    wide = sym.astype(jnp.float32)
    norm_one, var_one = normalize(wide, count)
    z_one = gain_one[:, None, None] * norm_one
    act_one = elu(z_one).astype(jnp.bfloat16)
    row_ids = lax.dynamic_slice_in_dim(chain[0], lax.axis_index("row") * side, side)
    col_ids = lax.dynamic_slice_in_dim(chain[0], lax.axis_index("col") * side, side)
    cross = (row_ids[:, None] != col_ids[None, :]).astype(jnp.float32)
    padded_one = widen(act_one)
    hid = (
        dilated_convolve(padded_one, act_one.shape, w_one, dilation[0])
        + inter_bias[:, None, None] * cross[None]
    )
    norm_two, var_two = normalize(hid, count)
    z_two = gain_two[:, None, None] * norm_two
    act_two = elu(z_two).astype(jnp.bfloat16)
    padded_two = widen(act_two)
    upd = dilated_convolve(padded_two, act_two.shape, w_two, dilation[1])
    cot_wide = cotangent[0].astype(jnp.float32)
    loss = jnp.sum((wide + upd) * cot_wide) / length
    g_upd = (cot_wide / length).astype(jnp.bfloat16)
    grad_two = kernel_weight_gradient(g_upd, padded_two, dilation[1])
    d_act_two = convolve_backward(g_upd, w_two, dilation[1])
    d_z_two = d_act_two * elu_slope(z_two)
    grad_g_two = jnp.sum(d_z_two * norm_two, axis=(1, 2))
    d_norm_two = d_z_two * gain_two[:, None, None]
    sums = paired_total(
        jnp.sum(d_norm_two, axis=(1, 2)), jnp.sum(d_norm_two * norm_two, axis=(1, 2))
    )
    mean_a = sums[0] / count
    mean_b = sums[1] / count
    d_hid = (d_norm_two - mean_a[:, None, None] - norm_two * mean_b[:, None, None]) * lax.rsqrt(
        var_two + eps
    )[:, None, None]
    grad_int = jnp.sum(d_hid * cross[None], axis=(1, 2))
    d_hid_low = d_hid.astype(jnp.bfloat16)
    grad_one = kernel_weight_gradient(d_hid_low, padded_one, dilation[0])
    d_act_one = convolve_backward(d_hid_low, w_one, dilation[0])
    grad_g_one = jnp.sum(d_act_one * elu_slope(z_one) * norm_one, axis=(1, 2))
    totals = lax.psum(
        (grad_one, grad_two, grad_g_one, grad_g_two, grad_int, loss), ("row", "col", "dp")
    )
    return (totals[0], totals[1], totals[2], totals[3], totals[4], totals[5])


def solution(mesh):
    in_specs = (
        P("dp", None, "row", "col"),
        P("dp", None, "row", "col"),
        P("dp", None),
        P(),
        P(),
        P(),
        P(),
        P(),
        P(),
    )
    out_specs = (P(), P(), P(), P(), P(), P())
    return jax.shard_map(local, mesh=mesh, in_specs=in_specs, out_specs=out_specs, check_vma=False)
```

profile of v0, /device:TPU:0, one launch (start us, length us, event | category | flops | bytes accessed | tf_op | source)
XLA Modules:
  0.0 701.5 jit_solution(5183082801833041562)
XLA Ops:
  7.2 4.3 copy.340
  11.5 4.6 all-to-all-start
  23.6 18.8 %all-to-all-done = bf16[1,1,64,128,128]{4,2,1,0,3:T(8,128)(2,1)} async-done(((bf16[1,1,64,128,128]{4,2,1,0,3:T(8,128)(2,1)}), bf16[1,1,64,128,128]{4,2,1,0,3:T(8,128)(2,1)}, u32[]{:S(2)}, u32[]{:S(2)}) %all-to-all-start) | async-done | bytes 2097184 | tf_op jit(solution)/shard_map/all_to_all | solution.py:121
  42.4 4.3 copy.339
  46.7 5.8 all-to-all-start.1
  52.6 4.3 fusion.4
  63.9 4.3 copy.72
  77.3 3.9 copy.64
  81.2 5.3 collective-permute-start.2
  86.6 4.2 copy.67
  91.9 5.0 copy.66
  96.9 8.6 %pad_maximum_fusion = bf16[64,144,144]{2,0,1:T(8,128)(2,1)} fusion(bf16[64,144,8]{2,0,1:T(8,128)(2,1)} %copy.67, bf16[64,8,128]{2,0,1:T(8,128)(2,1)S(1)} %collective-permute-done.1, bf16[64,128,128]{2,0,1:T(8,128)(2,1)S(1)} %fusion.2, bf16[64,8,128]{2,0,1:T(8,128)(2,1)S(1)} %collective-permute-done, bf16[64,144,8]{2,0,1:T(8,128)(2,1)} %copy.66), kind=kLoop, calls=%fused_computation.46 | loop fusion | flops 13271040 | bytes 5308416 | tf_op jit(solution)/shard_map/concatenate | solution.py:19
  105.5 21.0 %dynamic-slice_bitcast_fusion.8 = (bf16[128,8,8,128]{3,2,1,0:T(8,128)(2,1)}, bf16[128,8,8,128]{3,2,1,0:T(8,128)(2,1)}, bf16[128,8,8,128]{3,2,1,0:T(8,128)(2,1)},...) fusion(bf16[64,144,144]{2,0,1:T(8,128)(2,1)} %pad_maximum_fusio, ...), kind=kLoop, calls=%fused_computation.182 | loop fusion | bytes 33554440
  130.9 4.6 all-to-all-start.2
  145.0 16.3 %all-to-all-done.2 = bf16[1,4,64,32,128]{4,3,2,0,1:T(8,128)(2,1)} async-done(((bf16[1,4,64,32,128]{4,3,2,0,1:T(8,128)(2,1)}), bf16[1,4,64,32,128]{4,3,2,0,1:T(8,128)(2,1)}, u32[]{:S(2)}, u32[]{:S(2)}) %all-to-all-start.2) | async-done | bytes 2097184 | tf_op jit(solution)/shard_map/all_to_all | solution.py:127
  161.2 4.1 bitcast_convert_fusion
  165.4 5.5 copy.82
  170.9 5.2 convert_reduce_fusion
  176.1 48.7 %all-reduce.4 = (f32[64]{0:T(128)S(1)}, f32[64]{0:T(128)S(1)}) all-reduce(f32[64]{0:T(128)S(1)} %get-tuple-element.14, f32[64]{0:T(128)S(1)} %get-tuple-element.13), channel_id=1, replica_groups=mesh['row'=4,'col'=4,'dp'=2] {'row','col'}, use_global_device_ids=true, to_apply=%region_3.0 | all-reduce | flops 128 | bytes 1024 | tf_op jit(solution)/shard_map/psum | solution.py:103
  232.5 4.3 convolution_add_fusion.26
  245.9 3.9 copy.83
  249.8 5.3 collective-permute-start.6
  255.1 5.5 convolution_add_fusion.25
  260.6 4.1 copy.86
  264.8 5.0 copy.85
  269.8 8.6 %pad_maximum_fusion.1 = bf16[64,144,144]{2,0,1:T(8,128)(2,1)} fusion(bf16[64,144,8]{2,0,1:T(8,128)(2,1)} %copy.86, bf16[64,8,128]{2,0,1:T(8,128)(2,1)S(1)} %collective-permute-done.5, bf16[64,128,128]{2,0,1:T(8,128)(2,1)S(1)} %fusion.5, bf16[64,8,128]{2,0,1:T(8,128)(2,1)S(1)} %collective-permute-done.4, bf16[64,144,8]{2,0,1:T(8,128)(2,1)} %copy.85), kind=kLoop, calls=%fused_computation.47 | loop fusion | flops 13271040 | bytes 5308416 | tf_op jit(solution)/shard_map/concatenate | solution.py:19
  278.4 20.6 %dynamic-slice_bitcast_fusion.22 = (bf16[128,8,8,128]{3,2,1,0:T(8,128)(2,1)}, bf16[128,8,8,128]{3,2,1,0:T(8,128)(2,1)S(1)}, bf16[128,8,8,128]{3,2,1,0:T(8,128)(2...) fusion(bf16[64,144,144]{2,0,1:T(8,128)(2,1)} %pad_maximum_fusio, ...), kind=kLoop, calls=%fused_computation.211 | loop fusion | bytes 33554440
  315.7 29.7 %all-reduce.3 = (f32[64]{0:T(128)S(1)}, f32[64]{0:T(128)S(1)}) all-reduce(f32[64]{0:T(128)S(1)} %get-tuple-element.10, f32[64]{0:T(128)S(1)} %get-tuple-element.9), channel_id=1, replica_groups=mesh['row'=4,'col'=4,'dp'=2] {'row','col'}, use_global_device_ids=true, to_apply=%region_7.8 | all-reduce | flops 128 | bytes 1024 | tf_op jit(solution)/shard_map/psum | solution.py:103
  345.4 7.1 %multiply_reduce_fusion.1 = (f32[64]{0:T(128)}, f32[64]{0:T(128)S(1)}, f32[64]{0:T(128)S(1)}, f32[16384,64]{0,1:T(8,128)}) fusion(f32[64]{0:T(128)S(1)} %copy-done.51, f32[64]{0:T(128)S(1)} %get-tuple-element.84, f32[64]{0:T(128)S(1)} %get-tuple-element.83, f32[16384]{0:T(1024)S(1)} %fusion.247, f32[64]{0:T(128)S(1)} %copy-done.48, ...), kind=kOutput, calls=%fused_computation.80 | convolution fusion | flops 150994752 | bytes 14764800 | tf_op jit(solution)/shard_map/dot_general | solution.py:71
  352.5 32.1 %all-reduce.2 = (f32[64]{0:T(128)S(1)}, f32[64]{0:T(128)S(1)}) all-reduce(f32[64]{0:T(128)S(1)} %get-tuple-element.8, f32[64]{0:T(128)S(1)} %get-tuple-element.7), channel_id=1, replica_groups=mesh['row'=4,'col'=4,'dp'=2] {'row','col'}, use_global_device_ids=true, to_apply=%region_11.12 | all-reduce | flops 128 | bytes 1024 | tf_op jit(solution)/shard_map/psum | solution.py:103
  384.6 7.4 %multiply_reduce_fusion = (f32[64]{0:T(128)}, bf16[64,16384]{1,0:T(8,128)(2,1)}, bf16[8,128,8,128]{3,2,1,0:T(8,128)(2,1)}) fusion(f32[16384]{0:T(1024)S(1)} %fusion.247, f32[64]{0:T(128)S(1)} %get-tuple-element.91, f32[64]{0:T(128)S(1)} %get-tuple-element.92, f32[64]{0:T(128)S(1)} %get-tuple-element.84, f32[64]{0:T(128)S(1)} %get-tuple-element.83, ...), kind=kLoop, calls=%fused_computation.79 | loop fusion | flops 20971456 | bytes 12650240 | tf_op jit(solution)/shard_map/reduce_sum | solution.py:165
  416.6 4.6 copy.99
  422.4 4.6 copy.98
  427.0 5.2 collective-permute-start.10
  441.0 4.6 copy.103
  445.6 5.4 collective-permute-start.14
  451.0 5.0 copy.101
  456.0 5.0 copy.100
  461.0 7.7 %pad_maximum_fusion.2 = bf16[64,144,144]{2,0,1:T(8,128)(2,1)S(1)} fusion(bf16[64,144,8]{2,0,1:T(8,128)(2,1)} %copy.101, bf16[64,8,128]{2,0,1:T(8,128)(2,1)S(1)} %collective-permute-done.9, bf16[64,128,128]{2,0,1:T(8,128)(2,1)} %copy-done.7, bf16[64,8,128]{2,0,1:T(8,128)(2,1)S(1)} %collective-permute-done.8, bf16[64,144,8]{2,0,1:T(8,128)(2,1)} %copy.100), kind=kLoop, calls=%fused_computation.48 | loop fusion | flops 13271040 | bytes 5308416 | tf_op jit(solution)/shard_map/concatenate | solution.py:19
  472.7 21.5 %dynamic-slice_bitcast_fusion.16 = (bf16[128,8,8,128]{3,2,1,0:T(8,128)(2,1)}, bf16[128,8,8,128]{3,2,1,0:T(8,128)(2,1)}, bf16[128,8,8,128]{3,2,1,0:T(8,128)(2,1)}...) fusion(bf16[64,144,144]{2,0,1:T(8,128)(2,1)} %copy-done, ...), kind=kLoop, calls=%fused_computation.191 | loop fusion | bytes 33554440
  494.2 4.7 fusion.155
  517.2 4.4 convolution_add_fusion.4
  523.5 4.2 copy.106
  527.7 5.0 copy.105
  532.7 8.6 %pad_maximum_fusion.3 = bf16[64,144,144]{2,0,1:T(8,128)(2,1)} fusion(bf16[64,144,8]{2,0,1:T(8,128)(2,1)} %copy.106, bf16[64,8,128]{2,0,1:T(8,128)(2,1)S(1)} %collective-permute-done.13, bf16[64,128,128]{2,0,1:T(8,128)(2,1)S(1)} %get-tuple-element.64, bf16[64,8,128]{2,0,1:T(8,128)(2,1)S(1)} %collective-permute-done.12, bf16[64,144,8]{2,0,1:T(8,128)(2,1)} %copy.105), kind=kLoop, calls=%fused_computation.49 | loop fusion | flops 13271040 | bytes 5308416 | tf_op jit(solution)/shard_map/concatenate | solution.py:19
  541.3 21.0 %dynamic-slice_bitcast_fusion = (bf16[128,8,8,128]{3,2,1,0:T(8,128)(2,1)}, bf16[128,8,8,128]{3,2,1,0:T(8,128)(2,1)}, bf16[128,8,8,128]{3,2,1,0:T(8,128)(2,1)}, b...) fusion(bf16[64,144,144]{2,0,1:T(8,128)(2,1)} %pad_maximum_fusio, ...), kind=kLoop, calls=%fused_computation.173 | loop fusion | bytes 33554440
  592.4 37.8 %all-reduce = (f32[64]{0:T(128)}, f32[64]{0:T(128)}, f32[64]{0:T(128)}, f32[]{:T(128)}) all-reduce(f32[64]{0:T(128)S(1)} %get-tuple-element.12, f32[64]{0:T(128)S(1)} %copy-done.58, f32[64]{0:T(128)S(1)} %copy-done.55, f32[]{:T(128)S(6)} %div.41), channel_id=1, replica_groups=mesh['row'=4,'col'=4,'dp'=2] {'row','col','dp'}, use_global_device_ids=true, to_apply=%region_15.16 | all-reduce | flops 193 | bytes 1544 | tf_op jit(solution)/shard_map/psum | solution.py:170
  630.3 60.8 %all-reduce.7.cloned.1.call-done = (f32[9,64,64]{2,1,0:T(8,128)}, f32[9,64,64]{2,1,0:T(8,128)}) async-done(((f32[9,64,64]{2,1,0:T(8,128)}, f32[9,64,64]{2,1,0:T(8,128)}), (f32[9,64,64]{2,1,0:T(8,128)}, f32[9,64,64]{2,1,0:T(8,128)})) %all-reduce.7.cloned.1.call-update) | async-done | bytes 294928 | tf_op jit(solution)/shard_map/psum | solution.py:170
  (232 shorter events, 156.6 us)
Async XLA Ops:
  11.5 11.9 %copy-start.57 = (s32[1,512]{1,0:T(1,128)S(1)}, s32[1,512]{1,0:T(1,128)}, u32[]{:S(2)}) copy-start(s32[1,512]{1,0:T(1,128)} %param.11) | copy-start | bytes 6148
  11.5 31.0 %all-to-all-start = ((bf16[1,1,64,128,128]{4,2,1,0,3:T(8,128)(2,1)}), bf16[1,1,64,128,128]{4,2,1,0,3:T(8,128)(2,1)}, u32[]{:S(2)}, u32[]{:S(2)}) async-start(bf16[1,1,64,128,128]{4,2,1,0,3:T(8,128)(2,1)} %bitcast.515), calls=%async_computation | async-start | bytes 4194304 | tf_op jit(solution)/shard_map/all_to_all | solution.py:121
  19.0 49.2 %collective-permute-start.1 = (bf16[64,8,128]{2,0,1:T(8,128)(2,1)S(1)}, bf16[64,8,128]{2,0,1:T(8,128)(2,1)S(1)}, u32[]{:S(2)}, u32[]{:S(2)}) collective-permute-start(bf16[64,8,128]{2,0,1:T(8,128)(2,1)S(1)} %get-tuple-element.80), channel_id=1, source_target_pairs={{8,0},{16,8},{24,16},{9,1},{17,9},{25,17},{10,2},{18,10},{26,18},{... | collective-permute-start | bytes 393224 | tf_op jit(solution)/shard_map/ppermute | solution.py:18
  20.3 47.9 %collective-permute-start = (bf16[64,8,128]{2,0,1:T(8,128)(2,1)S(1)}, bf16[64,8,128]{2,0,1:T(8,128)(2,1)S(1)}, u32[]{:S(2)}, u32[]{:S(2)}) collective-permute-start(bf16[64,8,128]{2,0,1:T(8,128)(2,1)S(1)} %get-tuple-element.79), channel_id=1, source_target_pairs={{0,8},{8,16},{16,24},{1,9},{9,17},{17,25},{2,10},{10,18},{18,26},{... | collective-permute-start | bytes 393224 | tf_op jit(solution)/shard_map/ppermute | solution.py:15
  46.7 10.1 %copy-start.56 = (s32[2]{0:T(128)S(1)}, s32[2]{0:T(128)}, u32[]{:S(2)}) copy-start(s32[2]{0:T(128)} %param.12) | copy-start | bytes 28
  46.7 84.1 %all-to-all-start.1 = ((bf16[4,1,64,32,128]{4,3,2,1,0:T(8,128)(2,1)}), bf16[4,1,64,32,128]{4,3,2,1,0:T(8,128)(2,1)}, u32[]{:S(2)}, u32[]{:S(2)}) async-start(bf16[4,1,64,32,128]{4,3,2,1,0:T(8,128)(2,1)} %bitcast.520), calls=%async_computation.1 | async-start | bytes 4194304 | tf_op jit(solution)/shard_map/all_to_all | solution.py:120
  75.9 10.7 %collective-permute-start.3 = (bf16[64,144,8]{1,2,0:T(8,128)(2,1)S(1)}, bf16[64,144,8]{1,2,0:T(8,128)(2,1)S(1)}, u32[]{:S(2)}, u32[]{:S(2)}) collective-permute-start(bf16[64,144,8]{1,2,0:T(8,128)(2,1)S(1)} %copy.65), channel_id=1, source_target_pairs={{2,0},{4,2},{6,4},{3,1},{5,3},{7,5},{10,8},{12,10},{14,12},{11,9},... | collective-permute-start | bytes 442376 | tf_op jit(solution)/shard_map/ppermute | solution.py:18
  81.2 10.7 %collective-permute-start.2 = (bf16[64,144,8]{1,2,0:T(8,128)(2,1)S(1)}, bf16[64,144,8]{1,2,0:T(8,128)(2,1)}, u32[]{:S(2)}, u32[]{:S(2)}) collective-permute-start(bf16[64,144,8]{1,2,0:T(8,128)(2,1)S(1)} %copy.64), channel_id=1, source_target_pairs={{0,2},{2,4},{4,6},{1,3},{3,5},{5,7},{8,10},{10,12},{12,14},{9,11},... | collective-permute-start | bytes 442376 | tf_op jit(solution)/shard_map/ppermute | solution.py:15
  105.5 21.0 %copy-start.44 = (bf16[9,64,64]{2,1,0:T(8,128)(2,1)S(1)}, bf16[9,64,64]{2,1,0:T(8,128)(2,1)}, u32[]{:S(2)}) copy-start(bf16[9,64,64]{2,1,0:T(8,128)(2,1)} %param.14) | copy-start | bytes 221188
  130.9 4.9 copy-start.29
  130.9 30.3 %all-to-all-start.2 = ((bf16[1,4,64,32,128]{4,3,2,0,1:T(8,128)(2,1)}), bf16[1,4,64,32,128]{4,3,2,0,1:T(8,128)(2,1)}, u32[]{:S(2)}, u32[]{:S(2)}) async-start(bf16[1,4,64,32,128]{4,3,2,0,1:T(8,128)(2,1)} %bitcast.21), calls=%async_computation.2 | async-start | bytes 4194304 | tf_op jit(solution)/shard_map/all_to_all | solution.py:127
  135.5 555.6 %all-reduce.7.cloned.1.call-start = ((), (), s32[]{:S(2)}) async-start(), calls=%async_computation.3 | async-start | bytes 1179648 | tf_op jit(solution)/shard_map/psum | solution.py:170
  135.7 3.1 copy-start.27
  165.4 5.5 copy-start.39
  170.9 53.9 %copy-start.53 = (f32[64]{0:T(128)S(1)}, f32[64]{0:T(128)}, u32[]{:S(2)}) copy-start(f32[64]{0:T(128)} %param.15) | copy-start | bytes 772
  224.7 7.7 %copy-start.14 = (f32[16384,64]{0,1:T(8,128)S(1)}, f32[16384,64]{0,1:T(8,128)}, u32[]{:S(2)}) copy-start(f32[16384,64]{0,1:T(8,128)} %convolution_add_fusion.27) | copy-start | bytes 12582916
  224.8 80.6 %copy-start.49 = (f32[64]{0:T(128)}, f32[64]{0:T(128)S(1)}, u32[]{:S(2)}) copy-start(f32[64]{0:T(128)S(1)} %get-tuple-element.88) | copy-start | bytes 772
  228.1 41.7 %copy-start.4 = (bf16[64,128,128]{2,0,1:T(8,128)(2,1)}, bf16[64,128,128]{2,0,1:T(8,128)(2,1)S(1)}, u32[]{:S(2)}) copy-start(bf16[64,128,128]{2,0,1:T(8,128)(2,1)S(1)} %fusion.5) | copy-start | bytes 6291460
  228.1 8.7 %collective-permute-start.5 = (bf16[64,8,128]{2,0,1:T(8,128)(2,1)S(1)}, bf16[64,8,128]{2,0,1:T(8,128)(2,1)S(1)}, u32[]{:S(2)}, u32[]{:S(2)}) collective-permute-start(bf16[64,8,128]{2,0,1:T(8,128)(2,1)S(1)} %get-tuple-element.78), channel_id=1, source_target_pairs={{8,0},{16,8},{24,16},{9,1},{17,9},{25,17},{10,2},{18,10},{26,18},{... | collective-permute-start | bytes 393224 | tf_op jit(solution)/shard_map/ppermute | solution.py:18
  229.4 7.4 %collective-permute-start.4 = (bf16[64,8,128]{2,0,1:T(8,128)(2,1)S(1)}, bf16[64,8,128]{2,0,1:T(8,128)(2,1)S(1)}, u32[]{:S(2)}, u32[]{:S(2)}) collective-permute-start(bf16[64,8,128]{2,0,1:T(8,128)(2,1)S(1)} %get-tuple-element.77), channel_id=1, source_target_pairs={{0,8},{8,16},{16,24},{1,9},{9,17},{17,25},{2,10},{10,18},{18,26},{... | collective-permute-start | bytes 393224 | tf_op jit(solution)/shard_map/ppermute | solution.py:15
  244.2 16.4 %collective-permute-start.7 = (bf16[64,144,8]{1,2,0:T(8,128)(2,1)S(1)}, bf16[64,144,8]{1,2,0:T(8,128)(2,1)S(1)}, u32[]{:S(2)}, u32[]{:S(2)}) collective-permute-start(bf16[64,144,8]{1,2,0:T(8,128)(2,1)S(1)} %copy.84), channel_id=1, source_target_pairs={{2,0},{4,2},{6,4},{3,1},{5,3},{7,5},{10,8},{12,10},{14,12},{11,9},... | collective-permute-start | bytes 442376 | tf_op jit(solution)/shard_map/ppermute | solution.py:18
  249.8 14.9 %collective-permute-start.6 = (bf16[64,144,8]{1,2,0:T(8,128)(2,1)S(1)}, bf16[64,144,8]{1,2,0:T(8,128)(2,1)}, u32[]{:S(2)}, u32[]{:S(2)}) collective-permute-start(bf16[64,144,8]{1,2,0:T(8,128)(2,1)S(1)} %copy.83), channel_id=1, source_target_pairs={{0,2},{2,4},{4,6},{1,3},{3,5},{5,7},{8,10},{10,12},{12,14},{9,11},... | collective-permute-start | bytes 442376 | tf_op jit(solution)/shard_map/ppermute | solution.py:15
  278.4 20.6 %copy-start.45 = (bf16[9,64,64]{2,1,0:T(8,128)(2,1)S(1)}, bf16[9,64,64]{2,1,0:T(8,128)(2,1)}, u32[]{:S(2)}) copy-start(bf16[9,64,64]{2,1,0:T(8,128)(2,1)} %param.13) | copy-start | bytes 221188
  312.4 33.1 %copy-start.42 = (bf16[128,8,8,128]{3,2,1,0:T(8,128)(2,1)S(1)}, bf16[128,8,8,128]{3,2,1,0:T(8,128)(2,1)}, u32[]{:S(2)}) copy-start(bf16[128,8,8,128]{3,2,1,0:T(8,128)(2,1)} %get-tuple-element.54) | copy-start | bytes 6291460
  312.4 33.1 %copy-start.51 = (f32[64]{0:T(128)S(1)}, f32[64]{0:T(128)}, u32[]{:S(2)}) copy-start(f32[64]{0:T(128)} %param.16) | copy-start | bytes 772
  384.6 7.4 %copy-start.2 = (f32[16384,64]{0,1:T(8,128)S(1)}, f32[16384,64]{0,1:T(8,128)}, u32[]{:S(2)}) copy-start(f32[16384,64]{0,1:T(8,128)} %get-tuple-element.89) | copy-start | bytes 12582916
  384.6 7.4 %copy-start.15 = (f32[16384,64]{0,1:T(8,128)S(1)}, f32[16384,64]{0,1:T(8,128)}, u32[]{:S(2)}) copy-start(f32[16384,64]{0,1:T(8,128)} %get-tuple-element.90) | copy-start | bytes 12582916
  384.6 10.4 %slice-start = ((s8[4718592]{0:T(1024)(128)(4,1)}), s8[524288]{0:T(1024)(128)(4,1)S(1)}, s32[]{:S(2)}) async-start(s8[4718592]{0:T(1024)(128)(4,1)} %bitcast.516), calls=%async_computation.4 | async-start | bytes 1048576
  392.0 3.0 slice-start.1
  395.0 18.0 %copy-start.7 = (bf16[64,128,128]{2,0,1:T(8,128)(2,1)}, bf16[64,128,128]{2,0,1:T(8,128)(2,1)S(1)}, u32[]{:S(2)}) copy-start(bf16[64,128,128]{2,0,1:T(8,128)(2,1)S(1)} %get-tuple-element.63) | copy-start | bytes 6291460
  403.8 12.8 %copy-start.46 = (f32[9,64,64]{2,1,0:T(8,128)}, f32[9,64,64]{2,1,0:T(8,128)S(1)}, u32[]{:S(2)}) copy-start(f32[9,64,64]{2,1,0:T(8,128)S(1)} %fusion.197) | copy-start | bytes 442372
  403.9 9.1 %collective-permute-start.9 = (bf16[64,8,128]{2,0,1:T(8,128)(2,1)S(1)}, bf16[64,8,128]{2,0,1:T(8,128)(2,1)S(1)}, u32[]{:S(2)}, u32[]{:S(2)}) collective-permute-start(bf16[64,8,128]{2,0,1:T(8,128)(2,1)S(1)} %get-tuple-element.76), channel_id=1, source_target_pairs={{8,0},{16,8},{24,16},{9,1},{17,9},{25,17},{10,2},{18,10},{26,18},{... | collective-permute-start | bytes 393224 | tf_op jit(solution)/shard_map/ppermute | solution.py:18
  405.2 7.8 %collective-permute-start.8 = (bf16[64,8,128]{2,0,1:T(8,128)(2,1)S(1)}, bf16[64,8,128]{2,0,1:T(8,128)(2,1)S(1)}, u32[]{:S(2)}, u32[]{:S(2)}) collective-permute-start(bf16[64,8,128]{2,0,1:T(8,128)(2,1)S(1)} %get-tuple-element.75), channel_id=1, source_target_pairs={{0,8},{8,16},{16,24},{1,9},{9,17},{17,25},{2,10},{10,18},{18,26},{... | collective-permute-start | bytes 393224 | tf_op jit(solution)/shard_map/ppermute | solution.py:15
  408.2 24.0 %collective-permute-start.13 = (bf16[64,8,128]{2,0,1:T(8,128)(2,1)S(1)}, bf16[64,8,128]{2,0,1:T(8,128)(2,1)S(1)}, u32[]{:S(2)}, u32[]{:S(2)}) collective-permute-start(bf16[64,8,128]{2,0,1:T(8,128)(2,1)S(1)} %get-tuple-element.74), channel_id=1, source_target_pairs={{8,0},{16,8},{24,16},{9,1},{17,9},{25,17},{10,2},{18,10},{26,18},{... | collective-permute-start | bytes 393224 | tf_op jit(solution)/shard_map/ppermute | solution.py:18
  409.5 22.7 %collective-permute-start.12 = (bf16[64,8,128]{2,0,1:T(8,128)(2,1)S(1)}, bf16[64,8,128]{2,0,1:T(8,128)(2,1)S(1)}, u32[]{:S(2)}, u32[]{:S(2)}) collective-permute-start(bf16[64,8,128]{2,0,1:T(8,128)(2,1)S(1)} %get-tuple-element.73), channel_id=1, source_target_pairs={{0,8},{8,16},{16,24},{1,9},{9,17},{17,25},{2,10},{10,18},{18,26},{... | collective-permute-start | bytes 393224 | tf_op jit(solution)/shard_map/ppermute | solution.py:15
  421.1 29.8 %collective-permute-start.11 = (bf16[64,144,8]{1,2,0:T(8,128)(2,1)}, bf16[64,144,8]{1,2,0:T(8,128)(2,1)}, u32[]{:S(2)}, u32[]{:S(2)}) collective-permute-start(bf16[64,144,8]{1,2,0:T(8,128)(2,1)} %copy.99), channel_id=1, source_target_pairs={{2,0},{4,2},{6,4},{3,1},{5,3},{7,5},{10,8},{12,10},{14,12},{11,9},... | collective-permute-start | bytes 442376 | tf_op jit(solution)/shard_map/ppermute | solution.py:18
  427.0 29.0 %collective-permute-start.10 = (bf16[64,144,8]{1,2,0:T(8,128)(2,1)}, bf16[64,144,8]{1,2,0:T(8,128)(2,1)}, u32[]{:S(2)}, u32[]{:S(2)}) collective-permute-start(bf16[64,144,8]{1,2,0:T(8,128)(2,1)} %copy.98), channel_id=1, source_target_pairs={{0,2},{2,4},{4,6},{1,3},{3,5},{5,7},{8,10},{10,12},{12,14},{9,11},... | collective-permute-start | bytes 442376 | tf_op jit(solution)/shard_map/ppermute | solution.py:15
  439.7 83.8 %collective-permute-start.15 = (bf16[64,144,8]{1,2,0:T(8,128)(2,1)S(1)}, bf16[64,144,8]{1,2,0:T(8,128)(2,1)S(1)}, u32[]{:S(2)}, u32[]{:S(2)}) collective-permute-start(bf16[64,144,8]{1,2,0:T(8,128)(2,1)S(1)} %copy.104), channel_id=1, source_target_pairs={{2,0},{4,2},{6,4},{3,1},{5,3},{7,5},{10,8},{12,10},{14,12},{11,9},... | collective-permute-start | bytes 442376 | tf_op jit(solution)/shard_map/ppermute | solution.py:18
  445.6 82.1 %collective-permute-start.14 = (bf16[64,144,8]{1,2,0:T(8,128)(2,1)}, bf16[64,144,8]{1,2,0:T(8,128)(2,1)}, u32[]{:S(2)}, u32[]{:S(2)}) collective-permute-start(bf16[64,144,8]{1,2,0:T(8,128)(2,1)} %copy.103), channel_id=1, source_target_pairs={{0,2},{2,4},{4,6},{1,3},{3,5},{5,7},{8,10},{10,12},{12,14},{9,11},... | collective-permute-start | bytes 442376 | tf_op jit(solution)/shard_map/ppermute | solution.py:15
  461.0 7.8 %copy-start.10 = (bf16[1,64,128,128]{3,2,1,0:T(8,128)(2,1)S(1)}, bf16[1,64,128,128]{3,2,1,0:T(8,128)(2,1)}, u32[]{:S(2)}) copy-start(bf16[1,64,128,128]{3,2,1,0:T(8,128)(2,1)} %param.10) | copy-start | bytes 6291460
  494.2 4.8 copy-start.1
  494.2 8.3 %copy-start.11 = (bf16[1,64,128,128]{3,2,1,0:T(8,128)(2,1)S(1)}, bf16[1,64,128,128]{3,2,1,0:T(8,128)(2,1)}, u32[]{:S(2)}) copy-start(bf16[1,64,128,128]{3,2,1,0:T(8,128)(2,1)} %param.10) | copy-start | bytes 6291460
  494.2 8.3 %copy-start.43 = (bf16[8,128,8,128]{3,2,1,0:T(8,128)(2,1)S(1)}, bf16[8,128,8,128]{3,2,1,0:T(8,128)(2,1)}, u32[]{:S(2)}) copy-start(bf16[8,128,8,128]{3,2,1,0:T(8,128)(2,1)} %get-tuple-element.62) | copy-start | bytes 6291460
  506.5 3.7 copy-start.32
  523.5 17.8 %copy-start.47 = (f32[9,64,64]{2,1,0:T(8,128)}, f32[9,64,64]{2,1,0:T(8,128)S(1)}, u32[]{:S(2)}) copy-start(f32[9,64,64]{2,1,0:T(8,128)S(1)} %fusion.233) | copy-start | bytes 442372
  565.1 3.7 copy-start.18
  588.3 4.1 copy-start.55
  588.3 4.1 copy-start.58
  (33 other events, 60.2 us)
Sparse Core Ops, SparseCore 0:
  565.2 125.7 all-reduce.6
where the time goes:
time: 712 us; the launch traced here: 702 us
  local copies, waits for them, and re-layouts  212 us (30%)
  blocking collectives  148 us (21%)
  waiting for transfers between devices  97.1 us (14%)
  matrix products  93.4 us (13%)
  other arithmetic  68.4 us (10%)
  starting transfers between devices  59.9 us (8%)
  between operations  22.4 us (3%)
    unnamed x129, local copies, waits for them, and re-layouts  113 us
    psum x3, blocking collectives, paired_total(): return lax.psum((first, second), ('row', 'col'))  110 us
    psum x1, waiting for transfers between devices, local(): lax.psum((grad_one, grad_two, grad_g_one, grad_g_two, grad_int, loss), ('...  60.8 us
    psum x1, blocking collectives, local(): lax.psum((grad_one, grad_two, grad_g_one, grad_g_two, grad_int, loss), ('...  37.8 us
    dot_general x18, matrix products, convolve_backward(): jnp.dot(kernel_weights[step].T, window_slice.reshape(chans, -1), preferre...  37.6 us
    concatenate x8, other arithmetic, padded(): block = jnp.concatenate([low, block, high], axis=dim)  34.8 us
    ppermute x8, starting transfers between devices, padded(): lax.ppermute(lax.slice_in_dim(block, block.shape[dim] - width, None, axis...  33.8 us
    dot_general x18, matrix products, kernel_weight_gradient(): lax.dot_general(flat, window_slice.reshape(chans, -1), (((1,), (1,)), (()...  30.2 us
  transfers between devices with their start and end apart: 20, of which 4 were waited for; matrix products, arithmetic and copies ran while one was open for 30% of the time, Pallas kernels for 0%

commit v1 on v0

--- a/solution.py
+++ b/solution.py
@@ -100,7 +100,7 @@
 
 
 def paired_total(first, second):
-    return lax.psum((first, second), ("row", "col"))
+    return lax.psum(lax.psum((first, second), "col"), "row")
 
 
 def normalize(values, count):

time: 712 us -> 666 us (0.935)
  blocking collectives: 148 us -> 102 us
    psum x3 -> x6, blocking collectives: 110 us -> 63.3 us  [paired_total(): return lax.psum(lax.psum((first, second), 'col'), 'row')]
  transfers between devices with their start and end apart: 20 -> 20, of which waited for: 4 -> 4; matrix products, arithmetic and copies ran while one was open for 30% -> 32% of each run, Pallas kernels for 0% -> 0%
where the time goes in v1:
time: 666 us; the launch traced here: 656 us
  local copies, waits for them, and re-layouts  212 us (32%)
  blocking collectives  102 us (15%)
  waiting for transfers between devices  97.2 us (15%)
  matrix products  93.3 us (14%)
  other arithmetic  68.5 us (10%)
  starting transfers between devices  60.5 us (9%)
  between operations  22.4 us (3%)
    unnamed x129, local copies, waits for them, and re-layouts  113 us
    psum x6, blocking collectives, paired_total(): return lax.psum(lax.psum((first, second), 'col'), 'row')  63.3 us
    psum x1, waiting for transfers between devices, local(): lax.psum((grad_one, grad_two, grad_g_one, grad_g_two, grad_int, loss), ('...  60.9 us
    psum x1, blocking collectives, local(): lax.psum((grad_one, grad_two, grad_g_one, grad_g_two, grad_int, loss), ('...  38.2 us
    dot_general x18, matrix products, convolve_backward(): jnp.dot(kernel_weights[step].T, window_slice.reshape(chans, -1), preferre...  37.6 us
    concatenate x8, other arithmetic, padded(): block = jnp.concatenate([low, block, high], axis=dim)  34.8 us
    ppermute x8, starting transfers between devices, padded(): lax.ppermute(lax.slice_in_dim(block, block.shape[dim] - width, None, axis...  34.3 us
    dot_general x18, matrix products, kernel_weight_gradient(): lax.dot_general(flat, window_slice.reshape(chans, -1), (((1,), (1,)), (()...  30.2 us
  transfers between devices with their start and end apart: 20, of which 4 were waited for; matrix products, arithmetic and copies ran while one was open for 32% of the time, Pallas kernels for 0%

profile of v1, /device:TPU:0, one launch (start us, length us, event | category | flops | bytes accessed | tf_op | source)
XLA Modules:
  0.0 655.6 jit_solution(6386728948424034810)
XLA Ops:
  7.2 4.3 copy.340
  11.5 4.6 all-to-all-start
  23.6 18.8 %all-to-all-done = bf16[1,1,64,128,128]{4,2,1,0,3:T(8,128)(2,1)} async-done(((bf16[1,1,64,128,128]{4,2,1,0,3:T(8,128)(2,1)}), bf16[1,1,64,128,128]{4,2,1,0,3:T(8,128)(2,1)}, u32[]{:S(2)}, u32[]{:S(2)}) %all-to-all-start) | async-done | bytes 2097184 | tf_op jit(solution)/shard_map/all_to_all | solution.py:121
  42.5 4.3 copy.339
  46.8 5.8 all-to-all-start.1
  52.6 4.3 fusion.4
  63.9 4.3 copy.72
  81.3 5.3 collective-permute-start.2
  86.6 4.1 copy.67
  91.9 5.0 copy.66
  96.9 8.6 %pad_maximum_fusion = bf16[64,144,144]{2,0,1:T(8,128)(2,1)} fusion(bf16[64,144,8]{2,0,1:T(8,128)(2,1)} %copy.67, bf16[64,8,128]{2,0,1:T(8,128)(2,1)S(1)} %collective-permute-done.1, bf16[64,128,128]{2,0,1:T(8,128)(2,1)S(1)} %fusion.2, bf16[64,8,128]{2,0,1:T(8,128)(2,1)S(1)} %collective-permute-done, bf16[64,144,8]{2,0,1:T(8,128)(2,1)} %copy.66), kind=kLoop, calls=%fused_computation.46 | loop fusion | flops 13271040 | bytes 5308416 | tf_op jit(solution)/shard_map/concatenate | solution.py:19
  105.5 21.1 %dynamic-slice_bitcast_fusion.8 = (bf16[128,8,8,128]{3,2,1,0:T(8,128)(2,1)}, bf16[128,8,8,128]{3,2,1,0:T(8,128)(2,1)}, bf16[128,8,8,128]{3,2,1,0:T(8,128)(2,1)},...) fusion(bf16[64,144,144]{2,0,1:T(8,128)(2,1)} %pad_maximum_fusio, ...), kind=kLoop, calls=%fused_computation.182 | loop fusion | bytes 33554440
  131.0 4.6 all-to-all-start.2
  145.1 16.3 %all-to-all-done.2 = bf16[1,4,64,32,128]{4,3,2,0,1:T(8,128)(2,1)} async-done(((bf16[1,4,64,32,128]{4,3,2,0,1:T(8,128)(2,1)}), bf16[1,4,64,32,128]{4,3,2,0,1:T(8,128)(2,1)}, u32[]{:S(2)}, u32[]{:S(2)}) %all-to-all-start.2) | async-done | bytes 2097184 | tf_op jit(solution)/shard_map/all_to_all | solution.py:127
  165.5 5.5 copy.82
  171.0 5.2 convert_reduce_fusion
  176.2 27.4 %all-reduce.4 = (f32[64]{0:T(128)S(1)}, f32[64]{0:T(128)S(1)}) all-reduce(f32[64]{0:T(128)S(1)} %get-tuple-element.14, f32[64]{0:T(128)S(1)} %get-tuple-element.13), channel_id=1, replica_groups=mesh['row'=4,'col'=4,'dp'=2] {'col'}, use_global_device_ids=true, to_apply=%region_4.0 | all-reduce | flops 128 | bytes 1024 | tf_op jit(solution)/shard_map/psum | solution.py:103
  203.5 5.7 all-reduce.7
  217.0 4.3 convolution_add_fusion.26
  234.4 5.3 collective-permute-start.6
  239.7 5.5 convolution_add_fusion.25
  245.2 4.2 copy.86
  249.4 5.0 copy.85
  254.4 8.7 %pad_maximum_fusion.1 = bf16[64,144,144]{2,0,1:T(8,128)(2,1)} fusion(bf16[64,144,8]{2,0,1:T(8,128)(2,1)} %copy.86, bf16[64,8,128]{2,0,1:T(8,128)(2,1)S(1)} %collective-permute-done.5, bf16[64,128,128]{2,0,1:T(8,128)(2,1)S(1)} %fusion.5, bf16[64,8,128]{2,0,1:T(8,128)(2,1)S(1)} %collective-permute-done.4, bf16[64,144,8]{2,0,1:T(8,128)(2,1)} %copy.85), kind=kLoop, calls=%fused_computation.47 | loop fusion | flops 13271040 | bytes 5308416 | tf_op jit(solution)/shard_map/concatenate | solution.py:19
  263.0 20.7 %dynamic-slice_bitcast_fusion.22 = (bf16[128,8,8,128]{3,2,1,0:T(8,128)(2,1)}, bf16[128,8,8,128]{3,2,1,0:T(8,128)(2,1)S(1)}, bf16[128,8,8,128]{3,2,1,0:T(8,128)(2...) fusion(bf16[64,144,144]{2,0,1:T(8,128)(2,1)} %pad_maximum_fusio, ...), kind=kLoop, calls=%fused_computation.211 | loop fusion | bytes 33554440
  300.5 8.4 %all-reduce.3 = (f32[64]{0:T(128)S(1)}, f32[64]{0:T(128)S(1)}) all-reduce(f32[64]{0:T(128)S(1)} %get-tuple-element.10, f32[64]{0:T(128)S(1)} %get-tuple-element.9), channel_id=1, replica_groups=mesh['row'=4,'col'=4,'dp'=2] {'col'}, use_global_device_ids=true, to_apply=%region_10.11 | all-reduce | flops 128 | bytes 1024 | tf_op jit(solution)/shard_map/psum | solution.py:103
  308.9 5.6 all-reduce.6
  314.6 7.1 %multiply_reduce_fusion.1 = (f32[64]{0:T(128)}, f32[64]{0:T(128)S(1)}, f32[64]{0:T(128)S(1)}, f32[16384,64]{0,1:T(8,128)}) fusion(f32[64]{0:T(128)S(1)} %copy-done.51, f32[64]{0:T(128)S(1)} %get-tuple-element.90, f32[64]{0:T(128)S(1)} %get-tuple-element.89, f32[16384]{0:T(1024)S(1)} %fusion.247, f32[64]{0:T(128)S(1)} %copy-done.48, ...), kind=kOutput, calls=%fused_computation.80 | convolution fusion | flops 150994752 | bytes 14764800 | tf_op jit(solution)/shard_map/dot_general | solution.py:71
  321.6 10.3 %all-reduce.2 = (f32[64]{0:T(128)S(1)}, f32[64]{0:T(128)S(1)}) all-reduce(f32[64]{0:T(128)S(1)} %get-tuple-element.8, f32[64]{0:T(128)S(1)} %get-tuple-element.7), channel_id=1, replica_groups=mesh['row'=4,'col'=4,'dp'=2] {'col'}, use_global_device_ids=true, to_apply=%region_16.17 | all-reduce | flops 128 | bytes 1024 | tf_op jit(solution)/shard_map/psum | solution.py:103
  331.9 5.9 all-reduce.5
  337.8 7.4 %multiply_reduce_fusion = (f32[64]{0:T(128)}, bf16[64,16384]{1,0:T(8,128)(2,1)}, bf16[8,128,8,128]{3,2,1,0:T(8,128)(2,1)}) fusion(f32[16384]{0:T(1024)S(1)} %fusion.247, f32[64]{0:T(128)S(1)} %get-tuple-element.97, f32[64]{0:T(128)S(1)} %get-tuple-element.98, f32[64]{0:T(128)S(1)} %get-tuple-element.90, f32[64]{0:T(128)S(1)} %get-tuple-element.89, ...), kind=kLoop, calls=%fused_computation.79 | loop fusion | flops 20971456 | bytes 12650240 | tf_op jit(solution)/shard_map/reduce_sum | solution.py:165
  370.4 4.6 copy.99
  376.2 4.5 copy.98
  380.8 5.3 collective-permute-start.10
  394.8 4.6 copy.103
  399.4 5.4 collective-permute-start.14
  404.8 5.0 copy.101
  409.8 5.0 copy.100
  414.8 7.7 %pad_maximum_fusion.2 = bf16[64,144,144]{2,0,1:T(8,128)(2,1)S(1)} fusion(bf16[64,144,8]{2,0,1:T(8,128)(2,1)} %copy.101, bf16[64,8,128]{2,0,1:T(8,128)(2,1)S(1)} %collective-permute-done.9, bf16[64,128,128]{2,0,1:T(8,128)(2,1)} %copy-done.7, bf16[64,8,128]{2,0,1:T(8,128)(2,1)S(1)} %collective-permute-done.8, bf16[64,144,8]{2,0,1:T(8,128)(2,1)} %copy.100), kind=kLoop, calls=%fused_computation.48 | loop fusion | flops 13271040 | bytes 5308416 | tf_op jit(solution)/shard_map/concatenate | solution.py:19
  426.5 21.5 %dynamic-slice_bitcast_fusion.16 = (bf16[128,8,8,128]{3,2,1,0:T(8,128)(2,1)}, bf16[128,8,8,128]{3,2,1,0:T(8,128)(2,1)}, bf16[128,8,8,128]{3,2,1,0:T(8,128)(2,1)}...) fusion(bf16[64,144,144]{2,0,1:T(8,128)(2,1)} %copy-done, ...), kind=kLoop, calls=%fused_computation.191 | loop fusion | bytes 33554440
  448.0 4.7 fusion.155
  471.0 4.4 convolution_add_fusion.4
  477.3 4.1 copy.106
  481.4 5.0 copy.105
  486.4 8.6 %pad_maximum_fusion.3 = bf16[64,144,144]{2,0,1:T(8,128)(2,1)} fusion(bf16[64,144,8]{2,0,1:T(8,128)(2,1)} %copy.106, bf16[64,8,128]{2,0,1:T(8,128)(2,1)S(1)} %collective-permute-done.13, bf16[64,128,128]{2,0,1:T(8,128)(2,1)S(1)} %get-tuple-element.70, bf16[64,8,128]{2,0,1:T(8,128)(2,1)S(1)} %collective-permute-done.12, bf16[64,144,8]{2,0,1:T(8,128)(2,1)} %copy.105), kind=kLoop, calls=%fused_computation.49 | loop fusion | flops 13271040 | bytes 5308416 | tf_op jit(solution)/shard_map/concatenate | solution.py:19
  495.0 20.9 %dynamic-slice_bitcast_fusion = (bf16[128,8,8,128]{3,2,1,0:T(8,128)(2,1)}, bf16[128,8,8,128]{3,2,1,0:T(8,128)(2,1)}, bf16[128,8,8,128]{3,2,1,0:T(8,128)(2,1)}, b...) fusion(bf16[64,144,144]{2,0,1:T(8,128)(2,1)} %pad_maximum_fusio, ...), kind=kLoop, calls=%fused_computation.173 | loop fusion | bytes 33554440
  546.0 38.2 %all-reduce = (f32[64]{0:T(128)}, f32[64]{0:T(128)}, f32[64]{0:T(128)}, f32[]{:T(128)}) all-reduce(f32[64]{0:T(128)S(1)} %get-tuple-element.12, f32[64]{0:T(128)S(1)} %copy-done.58, f32[64]{0:T(128)S(1)} %copy-done.55, f32[]{:T(128)S(6)} %div.41), channel_id=1, replica_groups=mesh['row'=4,'col'=4,'dp'=2] {'row','col','dp'}, use_global_device_ids=true, to_apply=%region_21.22 | all-reduce | flops 193 | bytes 1544 | tf_op jit(solution)/shard_map/psum | solution.py:170
  584.3 60.9 %all-reduce.10.cloned.1.call-done = (f32[9,64,64]{2,1,0:T(8,128)}, f32[9,64,64]{2,1,0:T(8,128)}) async-done(((f32[9,64,64]{2,1,0:T(8,128)}, f32[9,64,64]{2,1,0:T(8,128)}), (f32[9,64,64]{2,1,0:T(8,128)}, f32[9,64,64]{2,1,0:T(8,128)})) %all-reduce.10.cloned.1.call-update) | async-done | bytes 294928 | tf_op jit(solution)/shard_map/psum | solution.py:170
  (235 shorter events, 169.2 us)
Async XLA Ops:
  11.5 11.9 %copy-start.57 = (s32[1,512]{1,0:T(1,128)S(1)}, s32[1,512]{1,0:T(1,128)}, u32[]{:S(2)}) copy-start(s32[1,512]{1,0:T(1,128)} %param.11) | copy-start | bytes 6148
  11.5 31.0 %all-to-all-start = ((bf16[1,1,64,128,128]{4,2,1,0,3:T(8,128)(2,1)}), bf16[1,1,64,128,128]{4,2,1,0,3:T(8,128)(2,1)}, u32[]{:S(2)}, u32[]{:S(2)}) async-start(bf16[1,1,64,128,128]{4,2,1,0,3:T(8,128)(2,1)} %bitcast.515), calls=%async_computation | async-start | bytes 4194304 | tf_op jit(solution)/shard_map/all_to_all | solution.py:121
  19.0 49.2 %collective-permute-start.1 = (bf16[64,8,128]{2,0,1:T(8,128)(2,1)S(1)}, bf16[64,8,128]{2,0,1:T(8,128)(2,1)S(1)}, u32[]{:S(2)}, u32[]{:S(2)}) collective-permute-start(bf16[64,8,128]{2,0,1:T(8,128)(2,1)S(1)} %get-tuple-element.86), channel_id=1, source_target_pairs={{8,0},{16,8},{24,16},{9,1},{17,9},{25,17},{10,2},{18,10},{26,18},{... | collective-permute-start | bytes 393224 | tf_op jit(solution)/shard_map/ppermute | solution.py:18
  20.3 47.9 %collective-permute-start = (bf16[64,8,128]{2,0,1:T(8,128)(2,1)S(1)}, bf16[64,8,128]{2,0,1:T(8,128)(2,1)S(1)}, u32[]{:S(2)}, u32[]{:S(2)}) collective-permute-start(bf16[64,8,128]{2,0,1:T(8,128)(2,1)S(1)} %get-tuple-element.85), channel_id=1, source_target_pairs={{0,8},{8,16},{16,24},{1,9},{9,17},{17,25},{2,10},{10,18},{18,26},{... | collective-permute-start | bytes 393224 | tf_op jit(solution)/shard_map/ppermute | solution.py:15
  46.8 10.1 %copy-start.56 = (s32[2]{0:T(128)S(1)}, s32[2]{0:T(128)}, u32[]{:S(2)}) copy-start(s32[2]{0:T(128)} %param.12) | copy-start | bytes 28
  46.8 84.2 %all-to-all-start.1 = ((bf16[4,1,64,32,128]{4,3,2,1,0:T(8,128)(2,1)}), bf16[4,1,64,32,128]{4,3,2,1,0:T(8,128)(2,1)}, u32[]{:S(2)}, u32[]{:S(2)}) async-start(bf16[4,1,64,32,128]{4,3,2,1,0:T(8,128)(2,1)} %bitcast.520), calls=%async_computation.1 | async-start | bytes 4194304 | tf_op jit(solution)/shard_map/all_to_all | solution.py:120
  75.9 10.7 %collective-permute-start.3 = (bf16[64,144,8]{1,2,0:T(8,128)(2,1)S(1)}, bf16[64,144,8]{1,2,0:T(8,128)(2,1)S(1)}, u32[]{:S(2)}, u32[]{:S(2)}) collective-permute-start(bf16[64,144,8]{1,2,0:T(8,128)(2,1)S(1)} %copy.65), channel_id=1, source_target_pairs={{2,0},{4,2},{6,4},{3,1},{5,3},{7,5},{10,8},{12,10},{14,12},{11,9},... | collective-permute-start | bytes 442376 | tf_op jit(solution)/shard_map/ppermute | solution.py:18
  81.3 10.7 %collective-permute-start.2 = (bf16[64,144,8]{1,2,0:T(8,128)(2,1)S(1)}, bf16[64,144,8]{1,2,0:T(8,128)(2,1)}, u32[]{:S(2)}, u32[]{:S(2)}) collective-permute-start(bf16[64,144,8]{1,2,0:T(8,128)(2,1)S(1)} %copy.64), channel_id=1, source_target_pairs={{0,2},{2,4},{4,6},{1,3},{3,5},{5,7},{8,10},{10,12},{12,14},{9,11},... | collective-permute-start | bytes 442376 | tf_op jit(solution)/shard_map/ppermute | solution.py:15
  105.5 21.1 %copy-start.44 = (bf16[9,64,64]{2,1,0:T(8,128)(2,1)S(1)}, bf16[9,64,64]{2,1,0:T(8,128)(2,1)}, u32[]{:S(2)}) copy-start(bf16[9,64,64]{2,1,0:T(8,128)(2,1)} %param.14) | copy-start | bytes 221188
  131.0 4.9 copy-start.29
  131.0 30.3 %all-to-all-start.2 = ((bf16[1,4,64,32,128]{4,3,2,0,1:T(8,128)(2,1)}), bf16[1,4,64,32,128]{4,3,2,0,1:T(8,128)(2,1)}, u32[]{:S(2)}, u32[]{:S(2)}) async-start(bf16[1,4,64,32,128]{4,3,2,0,1:T(8,128)(2,1)} %bitcast.21), calls=%async_computation.2 | async-start | bytes 4194304 | tf_op jit(solution)/shard_map/all_to_all | solution.py:127
  135.6 509.6 %all-reduce.10.cloned.1.call-start = ((), (), s32[]{:S(2)}) async-start(), calls=%async_computation.3 | async-start | bytes 1179648 | tf_op jit(solution)/shard_map/psum | solution.py:170
  135.8 3.1 copy-start.27
  165.5 5.5 copy-start.39
  171.0 38.3 %copy-start.53 = (f32[64]{0:T(128)S(1)}, f32[64]{0:T(128)}, u32[]{:S(2)}) copy-start(f32[64]{0:T(128)} %param.15) | copy-start | bytes 772
  209.3 7.7 %copy-start.14 = (f32[16384,64]{0,1:T(8,128)S(1)}, f32[16384,64]{0,1:T(8,128)}, u32[]{:S(2)}) copy-start(f32[16384,64]{0,1:T(8,128)} %convolution_add_fusion.27) | copy-start | bytes 12582916
  209.3 80.8 %copy-start.49 = (f32[64]{0:T(128)}, f32[64]{0:T(128)S(1)}, u32[]{:S(2)}) copy-start(f32[64]{0:T(128)S(1)} %get-tuple-element.94) | copy-start | bytes 772
  212.6 41.8 %copy-start.4 = (bf16[64,128,128]{2,0,1:T(8,128)(2,1)}, bf16[64,128,128]{2,0,1:T(8,128)(2,1)S(1)}, u32[]{:S(2)}) copy-start(bf16[64,128,128]{2,0,1:T(8,128)(2,1)S(1)} %fusion.5) | copy-start | bytes 6291460
  212.7 8.7 %collective-permute-start.5 = (bf16[64,8,128]{2,0,1:T(8,128)(2,1)S(1)}, bf16[64,8,128]{2,0,1:T(8,128)(2,1)S(1)}, u32[]{:S(2)}, u32[]{:S(2)}) collective-permute-start(bf16[64,8,128]{2,0,1:T(8,128)(2,1)S(1)} %get-tuple-element.84), channel_id=1, source_target_pairs={{8,0},{16,8},{24,16},{9,1},{17,9},{25,17},{10,2},{18,10},{26,18},{... | collective-permute-start | bytes 393224 | tf_op jit(solution)/shard_map/ppermute | solution.py:18
  214.0 7.4 %collective-permute-start.4 = (bf16[64,8,128]{2,0,1:T(8,128)(2,1)S(1)}, bf16[64,8,128]{2,0,1:T(8,128)(2,1)S(1)}, u32[]{:S(2)}, u32[]{:S(2)}) collective-permute-start(bf16[64,8,128]{2,0,1:T(8,128)(2,1)S(1)} %get-tuple-element.83), channel_id=1, source_target_pairs={{0,8},{8,16},{16,24},{1,9},{9,17},{17,25},{2,10},{10,18},{18,26},{... | collective-permute-start | bytes 393224 | tf_op jit(solution)/shard_map/ppermute | solution.py:15
  228.8 16.4 %collective-permute-start.7 = (bf16[64,144,8]{1,2,0:T(8,128)(2,1)S(1)}, bf16[64,144,8]{1,2,0:T(8,128)(2,1)S(1)}, u32[]{:S(2)}, u32[]{:S(2)}) collective-permute-start(bf16[64,144,8]{1,2,0:T(8,128)(2,1)S(1)} %copy.84), channel_id=1, source_target_pairs={{2,0},{4,2},{6,4},{3,1},{5,3},{7,5},{10,8},{12,10},{14,12},{11,9},... | collective-permute-start | bytes 442376 | tf_op jit(solution)/shard_map/ppermute | solution.py:18
  234.4 15.0 %collective-permute-start.6 = (bf16[64,144,8]{1,2,0:T(8,128)(2,1)S(1)}, bf16[64,144,8]{1,2,0:T(8,128)(2,1)}, u32[]{:S(2)}, u32[]{:S(2)}) collective-permute-start(bf16[64,144,8]{1,2,0:T(8,128)(2,1)S(1)} %copy.83), channel_id=1, source_target_pairs={{0,2},{2,4},{4,6},{1,3},{3,5},{5,7},{8,10},{10,12},{12,14},{9,11},... | collective-permute-start | bytes 442376 | tf_op jit(solution)/shard_map/ppermute | solution.py:15
  263.0 20.7 %copy-start.45 = (bf16[9,64,64]{2,1,0:T(8,128)(2,1)S(1)}, bf16[9,64,64]{2,1,0:T(8,128)(2,1)}, u32[]{:S(2)}) copy-start(bf16[9,64,64]{2,1,0:T(8,128)(2,1)} %param.13) | copy-start | bytes 221188
  297.1 17.4 %copy-start.42 = (bf16[128,8,8,128]{3,2,1,0:T(8,128)(2,1)S(1)}, bf16[128,8,8,128]{3,2,1,0:T(8,128)(2,1)}, u32[]{:S(2)}) copy-start(bf16[128,8,8,128]{3,2,1,0:T(8,128)(2,1)} %get-tuple-element.60) | copy-start | bytes 6291460
  297.1 17.4 %copy-start.51 = (f32[64]{0:T(128)S(1)}, f32[64]{0:T(128)}, u32[]{:S(2)}) copy-start(f32[64]{0:T(128)} %param.16) | copy-start | bytes 772
  337.8 7.4 %copy-start.2 = (f32[16384,64]{0,1:T(8,128)S(1)}, f32[16384,64]{0,1:T(8,128)}, u32[]{:S(2)}) copy-start(f32[16384,64]{0,1:T(8,128)} %get-tuple-element.95) | copy-start | bytes 12582916
  337.8 7.4 %copy-start.15 = (f32[16384,64]{0,1:T(8,128)S(1)}, f32[16384,64]{0,1:T(8,128)}, u32[]{:S(2)}) copy-start(f32[16384,64]{0,1:T(8,128)} %get-tuple-element.96) | copy-start | bytes 12582916
  337.8 10.4 %slice-start = ((s8[4718592]{0:T(1024)(128)(4,1)}), s8[524288]{0:T(1024)(128)(4,1)S(1)}, s32[]{:S(2)}) async-start(s8[4718592]{0:T(1024)(128)(4,1)} %bitcast.516), calls=%async_computation.4 | async-start | bytes 1048576
  345.2 3.0 slice-start.1
  348.2 18.6 %copy-start.7 = (bf16[64,128,128]{2,0,1:T(8,128)(2,1)}, bf16[64,128,128]{2,0,1:T(8,128)(2,1)S(1)}, u32[]{:S(2)}) copy-start(bf16[64,128,128]{2,0,1:T(8,128)(2,1)S(1)} %get-tuple-element.69) | copy-start | bytes 6291460
  357.0 13.4 %copy-start.46 = (f32[9,64,64]{2,1,0:T(8,128)}, f32[9,64,64]{2,1,0:T(8,128)S(1)}, u32[]{:S(2)}) copy-start(f32[9,64,64]{2,1,0:T(8,128)S(1)} %fusion.197) | copy-start | bytes 442372
  357.1 9.7 %collective-permute-start.9 = (bf16[64,8,128]{2,0,1:T(8,128)(2,1)S(1)}, bf16[64,8,128]{2,0,1:T(8,128)(2,1)S(1)}, u32[]{:S(2)}, u32[]{:S(2)}) collective-permute-start(bf16[64,8,128]{2,0,1:T(8,128)(2,1)S(1)} %get-tuple-element.82), channel_id=1, source_target_pairs={{8,0},{16,8},{24,16},{9,1},{17,9},{25,17},{10,2},{18,10},{26,18},{... | collective-permute-start | bytes 393224 | tf_op jit(solution)/shard_map/ppermute | solution.py:18
  358.4 8.4 %collective-permute-start.8 = (bf16[64,8,128]{2,0,1:T(8,128)(2,1)S(1)}, bf16[64,8,128]{2,0,1:T(8,128)(2,1)S(1)}, u32[]{:S(2)}, u32[]{:S(2)}) collective-permute-start(bf16[64,8,128]{2,0,1:T(8,128)(2,1)S(1)} %get-tuple-element.81), channel_id=1, source_target_pairs={{0,8},{8,16},{16,24},{1,9},{9,17},{17,25},{2,10},{10,18},{18,26},{... | collective-permute-start | bytes 393224 | tf_op jit(solution)/shard_map/ppermute | solution.py:15
  361.4 24.6 %collective-permute-start.13 = (bf16[64,8,128]{2,0,1:T(8,128)(2,1)S(1)}, bf16[64,8,128]{2,0,1:T(8,128)(2,1)S(1)}, u32[]{:S(2)}, u32[]{:S(2)}) collective-permute-start(bf16[64,8,128]{2,0,1:T(8,128)(2,1)S(1)} %get-tuple-element.80), channel_id=1, source_target_pairs={{8,0},{16,8},{24,16},{9,1},{17,9},{25,17},{10,2},{18,10},{26,18},{... | collective-permute-start | bytes 393224 | tf_op jit(solution)/shard_map/ppermute | solution.py:18
  362.7 23.3 %collective-permute-start.12 = (bf16[64,8,128]{2,0,1:T(8,128)(2,1)S(1)}, bf16[64,8,128]{2,0,1:T(8,128)(2,1)S(1)}, u32[]{:S(2)}, u32[]{:S(2)}) collective-permute-start(bf16[64,8,128]{2,0,1:T(8,128)(2,1)S(1)} %get-tuple-element.79), channel_id=1, source_target_pairs={{0,8},{8,16},{16,24},{1,9},{9,17},{17,25},{2,10},{10,18},{18,26},{... | collective-permute-start | bytes 393224 | tf_op jit(solution)/shard_map/ppermute | solution.py:15
  374.9 29.8 %collective-permute-start.11 = (bf16[64,144,8]{1,2,0:T(8,128)(2,1)}, bf16[64,144,8]{1,2,0:T(8,128)(2,1)}, u32[]{:S(2)}, u32[]{:S(2)}) collective-permute-start(bf16[64,144,8]{1,2,0:T(8,128)(2,1)} %copy.99), channel_id=1, source_target_pairs={{2,0},{4,2},{6,4},{3,1},{5,3},{7,5},{10,8},{12,10},{14,12},{11,9},... | collective-permute-start | bytes 442376 | tf_op jit(solution)/shard_map/ppermute | solution.py:18
  380.8 29.0 %collective-permute-start.10 = (bf16[64,144,8]{1,2,0:T(8,128)(2,1)}, bf16[64,144,8]{1,2,0:T(8,128)(2,1)}, u32[]{:S(2)}, u32[]{:S(2)}) collective-permute-start(bf16[64,144,8]{1,2,0:T(8,128)(2,1)} %copy.98), channel_id=1, source_target_pairs={{0,2},{2,4},{4,6},{1,3},{3,5},{5,7},{8,10},{10,12},{12,14},{9,11},... | collective-permute-start | bytes 442376 | tf_op jit(solution)/shard_map/ppermute | solution.py:15
  393.5 83.8 %collective-permute-start.15 = (bf16[64,144,8]{1,2,0:T(8,128)(2,1)S(1)}, bf16[64,144,8]{1,2,0:T(8,128)(2,1)S(1)}, u32[]{:S(2)}, u32[]{:S(2)}) collective-permute-start(bf16[64,144,8]{1,2,0:T(8,128)(2,1)S(1)} %copy.104), channel_id=1, source_target_pairs={{2,0},{4,2},{6,4},{3,1},{5,3},{7,5},{10,8},{12,10},{14,12},{11,9},... | collective-permute-start | bytes 442376 | tf_op jit(solution)/shard_map/ppermute | solution.py:18
  399.4 82.1 %collective-permute-start.14 = (bf16[64,144,8]{1,2,0:T(8,128)(2,1)}, bf16[64,144,8]{1,2,0:T(8,128)(2,1)}, u32[]{:S(2)}, u32[]{:S(2)}) collective-permute-start(bf16[64,144,8]{1,2,0:T(8,128)(2,1)} %copy.103), channel_id=1, source_target_pairs={{0,2},{2,4},{4,6},{1,3},{3,5},{5,7},{8,10},{10,12},{12,14},{9,11},... | collective-permute-start | bytes 442376 | tf_op jit(solution)/shard_map/ppermute | solution.py:15
  414.8 7.8 %copy-start.10 = (bf16[1,64,128,128]{3,2,1,0:T(8,128)(2,1)S(1)}, bf16[1,64,128,128]{3,2,1,0:T(8,128)(2,1)}, u32[]{:S(2)}) copy-start(bf16[1,64,128,128]{3,2,1,0:T(8,128)(2,1)} %param.10) | copy-start | bytes 6291460
  448.0 4.8 copy-start.1
  448.0 8.3 %copy-start.11 = (bf16[1,64,128,128]{3,2,1,0:T(8,128)(2,1)S(1)}, bf16[1,64,128,128]{3,2,1,0:T(8,128)(2,1)}, u32[]{:S(2)}) copy-start(bf16[1,64,128,128]{3,2,1,0:T(8,128)(2,1)} %param.10) | copy-start | bytes 6291460
  448.0 8.3 %copy-start.43 = (bf16[8,128,8,128]{3,2,1,0:T(8,128)(2,1)S(1)}, bf16[8,128,8,128]{3,2,1,0:T(8,128)(2,1)}, u32[]{:S(2)}) copy-start(bf16[8,128,8,128]{3,2,1,0:T(8,128)(2,1)} %get-tuple-element.68) | copy-start | bytes 6291460
  460.3 3.7 copy-start.32
  477.3 17.8 %copy-start.47 = (f32[9,64,64]{2,1,0:T(8,128)}, f32[9,64,64]{2,1,0:T(8,128)S(1)}, u32[]{:S(2)}) copy-start(f32[9,64,64]{2,1,0:T(8,128)S(1)} %fusion.233) | copy-start | bytes 442372
  518.7 3.7 copy-start.18
  542.0 4.1 copy-start.55
  542.0 4.1 copy-start.58
  (33 other events, 60.3 us)
Sparse Core Ops, SparseCore 0:
  518.9 126.2 all-reduce.9
